TPU v7x, 256 devices: a whole 4x4x8 slice. The times are simulated.
256 devices in a mesh: dp: 4 (over x), seq: 64 (over z, y, core).
Axes of the slice: x: 4, y: 4, z: 8, core: 2. Of those that a mesh axis runs over, the one named last changes fastest.
Arguments:
- hidden: bfloat16 [8, 16384, 4096], P('dp', 'seq'), may hold values from -6 to 6
- doc_lengths: int32 [8, 8], P('dp'), may hold values from 1 to 4096, 16384 in all within a row
- partner: int32 [64], replicated, may hold values from 0 to 63, as said below
- closing_layer_weight: float32 [4096], replicated, may hold values from 0.25 to 1.75
Outputs:
- hidden_grad: bfloat16 [8, 16384, 4096], P('dp', 'seq')
- loss_value: float32 [], replicated
Inputs may be any that keep to these rules, and one draw needn't show every extreme that they name: partner pairs the documents: partner[partner[i]] = i and partner[i] != i.
All inputs are finite; a program needn't handle non-finite values.
Results may differ from a plain program's by a relative error of at most 0.005.
Values sent between devices are 32-bit elements; how exact they have to be, the bound alone decides.
A program may use at most 64 MiB of HBM per device.

v0:
```python
import jax
import jax.numpy as jnp
from jax import lax
from jax.sharding import PartitionSpec as P

sharpness_divisor = 0.05
derivative_multiplier = 524288.0


def contrast(cosine_table, partner):
    count_docs = cosine_table.shape[0]
    embedding_lengths = jnp.sqrt(jnp.diagonal(cosine_table) + 1e-06)
    unnormalized_pair_affinity = (
        cosine_table / (embedding_lengths[:, None] * embedding_lengths[None, :]) / sharpness_divisor
    )
    rows_idx = jnp.arange(count_docs, dtype=jnp.int32)
    identity_selector = rows_idx[:, None] == rows_idx[None, :]
    weights = jnp.where(identity_selector, jnp.float32(0.0), jnp.exp(unnormalized_pair_affinity))
    log_total = jnp.log(jnp.sum(weights, axis=1))
    target = jnp.sum(
        jnp.where(
            rows_idx[None, :] == partner[:, None], unnormalized_pair_affinity, jnp.float32(0.0)
        ),
        axis=1,
    )
    return jnp.mean(log_total - target)


def contrast_grad(cosine_table, partner, first_doc, own_count):
    loss_value, back = jax.vjp(lambda matrix: contrast(matrix, partner), cosine_table)
    grad_gram = back(jnp.float32(1.0))[0]
    symmetric = grad_gram + grad_gram.T
    own_rows = lax.dynamic_slice_in_dim(symmetric, first_doc, own_count, 0)
    return (loss_value, own_rows)


def shards(hidden, doc_lengths, partner, closing_layer_weight):
    rows_dev, tok_count, width = hidden.shape
    docs_row = doc_lengths.shape[1]
    own_count = rows_dev * docs_row
    positions = lax.axis_index("seq") * tok_count + jnp.arange(tok_count, dtype=jnp.int32)
    finish = jnp.cumsum(doc_lengths, axis=1)
    starts = finish - doc_lengths
    member = (positions[None, None, :] >= starts[:, :, None]) & (
        positions[None, None, :] < finish[:, :, None]
    )
    float_values = hidden.astype(jnp.float32)
    inv_rms = lax.rsqrt(jnp.mean(float_values * float_values, axis=-1, keepdims=True) + 1e-06)
    normed = (float_values * inv_rms * closing_layer_weight).astype(jnp.bfloat16)
    partial_sums = jnp.einsum(
        "rdt,rtc->rdc", member.astype(jnp.bfloat16), normed, preferred_element_type=jnp.float32
    ).reshape(own_count, width)
    counts = doc_lengths.astype(jnp.float32).reshape(own_count)
    first_doc = lax.axis_index("dp") * own_count
    summed = lax.psum(partial_sums, "seq")
    own_mean = summed / counts[:, None]
    mean_pooled = lax.all_gather(own_mean, "dp", axis=0, tiled=True)
    cosine_table = jnp.dot(mean_pooled, mean_pooled.T, precision=lax.Precision.HIGHEST)
    loss_value, own_rows = contrast_grad(cosine_table, partner, first_doc, own_count)
    grad_pooled = jnp.dot(own_rows, mean_pooled, precision=lax.Precision.HIGHEST)
    scaled = (grad_pooled * (derivative_multiplier / counts)[:, None]).reshape(
        rows_dev, docs_row, width
    )
    grad_normed = jnp.einsum(
        "rdt,rdc->rtc", member.astype(jnp.float32), scaled, precision=lax.Precision.HIGHEST
    )
    weighted = closing_layer_weight * grad_normed
    inner = jnp.mean(float_values * weighted, axis=-1, keepdims=True)
    hidden_grad = (inv_rms * weighted - float_values * inv_rms**3 * inner).astype(jnp.bfloat16)
    return (hidden_grad, loss_value)


def solution(mesh):
    in_specs = (P("dp", "seq", None), P("dp", None), P(), P())
    out_specs = (P("dp", "seq", None), P())
    return jax.shard_map(shards, mesh=mesh, in_specs=in_specs, out_specs=out_specs, check_vma=False)
```

profile of v0, /device:TPU:1, one launch (start us, length us, event | category | flops | bytes accessed | tf_op | source)
XLA Modules:
  0.0 255.0 jit_solution(8203652161392011105)
XLA Ops:
  7.2 0.0 copy-start.1
  7.2 0.0 all-reduce.2.cloned.1.call-start
  7.2 0.0 copy-start
  7.2 3.1 %fusion = f32[2,256]{1,0:T(2,128)S(1)} fusion(bf16[2,256,4096]{2,1,0:T(8,128)(2,1)} %param.4), kind=kLoop, calls=%fused_computation.6 | loop fusion | flops 6290944 | bytes 4196352 | tf_op jit(solution)/shard_map/reduce_sum | solution.py:48
  10.3 0.9 reduce_window_sum.11
  11.2 0.8 fusion.30
  12.0 4.0 %convolution_bitcast_fusion = f32[16,4096]{1,0:T(8,128)} fusion(bf16[2,256,4096]{2,1,0:T(8,128)(2,1)} %param.4, f32[4096]{0:T(1024)} %param.7, f32[2,256]{1,0:T(2,128)S(1)} %get-tuple-element.15, s32[2,8]{1,0:T(2,128)S(1)} %reduce_window_sum.11, s32[2,8]{1,0:T(2,128)S(1)} %get-tuple-element.17, s32[256]{0:T(256)S(1)} %iota_add_fusion), kind=kOutput, calls=%fused_computation.13 | convolution fusion | flops 41955328 | bytes 4476032 | tf_op jit(solution)/shard_map/rdt,rtc->rdc/dot_general | solution.py:50
  16.0 0.0 all-reduce.2.cloned.1.call-update
  16.0 0.0 all-gather.2.cloned.1.call-start
  16.1 0.1 div.51
  16.1 179.2 %all-reduce.2.cloned.1.call-done = f32[16,4096]{1,0:T(8,128)} async-done(((f32[16,4096]{1,0:T(8,128)}), f32[16,4096]{1,0:T(8,128)}) %all-reduce.2.cloned.1.call-update) | async-done | bytes 262160 | tf_op jit(solution)/shard_map/psum | solution.py:55
  195.3 1.7 broadcast_divide_fusion
  197.1 0.0 all-gather.2.cloned.1.call-update
  197.1 23.5 %all-gather.2.cloned.1.call-done = f32[64,4096]{1,0:T(8,128)} async-done(((f32[16,4096]{1,0:T(8,128)}), f32[64,4096]{1,0:T(8,128)}) %all-gather.2.cloned.1.call-update) | async-done | bytes 1048592 | tf_op jit(solution)/shard_map/all_gather | solution.py:57
  220.6 2.5 fusion.31
  223.2 0.8 gather_fusion
  224.0 0.0 copy-done.1
  224.0 0.1 select_reduce_fusion
  224.1 0.6 subtract_reduce_fusion
  224.7 0.1 fusion.15
  224.8 0.1 multiply_reduce_fusion
  224.9 0.1 copy.8
  225.0 3.8 %scatter_fusion = f32[64,64]{1,0:T(8,128)S(1)} fusion(f32[64,64]{1,0:T(8,128)S(1)} %copy.8, s32[64]{0:T(128)S(1)} %fusion.27, f32[64]{0:T(128)S(1)} %multiply_multiply_fusion.2), kind=kCustom, calls=%fused_computation.1 | custom fusion | flops 64 | bytes 1280 | tf_op jit(solution)/shard_map/transpose(jvp(jit(diagonal)))/cond/branch_0_fun/scatter-add | solution.py:12
  228.8 0.1 copy.9
  228.9 1.8 fusion.7
  230.8 0.0 copy-done
  230.8 8.2 %fusion.6 = (f32[2,256]{1,0:T(2,128)S(1)}, f32[2,256,4096]{2,1,0:T(8,128)}) fusion(bf16[2,256,4096]{2,1,0:T(8,128)(2,1)} %param.4, f32[4096]{0:T(1024)S(1)} %copy-done, f32[2,8,4096]{2,1,0:T(8,128)S(1)} %fusion.7, s32[2,8]{1,0:T(2,128)S(1)} %reduce_window_sum.11, s32[2,8]{1,0:T(2,128)S(1)} %get-tuple-element.17, s32[256]{0:T(256)S(1)} %iota_add_fusion), kind=kOutput, calls=%fused_computation.12 | convolution fusion | flops 209726976 | bytes 12864640 | tf_op jit(solution)/shard_map/rdt,rdc->rtc/dot_general | solution.py:64
  239.7 7.3 %fusion.5 = bf16[2,256,4096]{2,1,0:T(8,128)(2,1)} fusion(bf16[2,256,4096]{2,1,0:T(8,128)(2,1)} %param.4, f32[2,256,4096]{2,1,0:T(8,128)} %get-tuple-element.21, f32[2,256]{1,0:T(2,128)S(1)} %broadcast_multiply_fusion, f32[2,256]{1,0:T(2,128)S(1)} %get-tuple-element.14, f32[4096]{0:T(1024)S(1)} %copy-done, f32[2,256]{1,0:T(2,128)S(1)} %get-tuple-element.15), kind=kLoop, calls=%fused_computation.11 | loop fusion | flops 14680064 | bytes 16799744 | tf_op jit(solution)/shard_map/convert_element_type | solution.py:69
  (8 shorter events, 0.1 us)
Async XLA Ops:
  7.2 216.8 %copy-start.1 = (s32[64]{0:T(128)S(1)}, s32[64]{0:T(128)}, u32[]{:S(2)}) copy-start(s32[64]{0:T(128)} %param.6) | copy-start | bytes 772
  7.2 188.2 %all-reduce.2.cloned.1.call-start = ((), (), s32[]{:S(2)}) async-start(), calls=%async_computation | async-start | bytes 524288 | tf_op jit(solution)/shard_map/psum | solution.py:55
  7.2 223.5 %copy-start = (f32[4096]{0:T(1024)S(1)}, f32[4096]{0:T(1024)}, u32[]{:S(2)}) copy-start(f32[4096]{0:T(1024)} %param.7) | copy-start | bytes 49156
  16.0 204.6 %all-gather.2.cloned.1.call-start = ((), (), s32[]{:S(2)}) async-start(), calls=%async_computation.1 | async-start | bytes 1310720 | tf_op jit(solution)/shard_map/all_gather | solution.py:57
Sparse Core Ops, SparseCore 0:
  16.1 179.1 all-reduce.1
  197.9 22.7 all-gather.1
where the time goes:
time: 255 us
  waiting for transfers between devices  203 us (80%)
  other arithmetic  18.6 us (7%)
  matrix products  16.6 us (7%)
  between operations  15.9 us (6%)
    psum x1, waiting for transfers between devices, shards(): summed = lax.psum(partial_sums, 'seq')  179 us
    all_gather x1, waiting for transfers between devices, shards(): mean_pooled = lax.all_gather(own_mean, 'dp', axis=0, tiled=True)  23.5 us
    dot_general x1, matrix products, shards(): jnp.einsum('rdt,rdc->rtc', member.astype(jnp.float32), scaled, precision=...  8.23 us
    convert_element_type x1, other arithmetic, shards(): (inv_rms * weighted - float_values * inv_rms ** 3 * inner).astype(jnp.bfl...  7.34 us
  transfers between devices with their start and end apart: 2, of which 2 were waited for; matrix products, arithmetic and copies ran while one was open for 0% of the time, Pallas kernels for 0%

commit v1 on v0

v1 whole, which is shorter than its diff:
```python
import jax
import jax.numpy as jnp
from jax import lax
from jax.experimental import pallas as pl
from jax.experimental.pallas import tpu as pltpu
from jax.sharding import PartitionSpec as P

MESH = pl.DeviceIdType.MESH
F32, BF16 = jnp.float32, jnp.bfloat16

SHARPNESS = 0.05
LOSS_SCALE = 524288.0
EPS = 1e-06

NX, NZ, NY, NCORE = 4, 8, 4, 2
CHIPS = NZ * NY
PLANE = NX * NY
D = 4096
DOCS_ROW = 8
NDOC = 64
TOK = 256
LANES = D // CHIPS
ZCOLS = LANES * NY
PARTS = 4
NEAR_FIRST = (0, 1, 7, 2, 6, 3, 5, 4)


def bounds(len_ref, row):
    along = len_ref[pl.ds(row, 1), :].astype(F32)
    k = lax.broadcasted_iota(jnp.int32, (DOCS_ROW, DOCS_ROW), 0)
    l = lax.broadcasted_iota(jnp.int32, (DOCS_ROW, DOCS_ROW), 1)
    spread = jnp.broadcast_to(along, (DOCS_ROW, DOCS_ROW))
    down = jnp.sum(jnp.where(k == l, spread, 0.0), axis=1, keepdims=True)
    finish_down = jnp.sum(jnp.where(l <= k, spread, 0.0), axis=1, keepdims=True)
    start_down = finish_down - down
    start_along = jnp.sum(jnp.where(k < l, jnp.broadcast_to(down, (DOCS_ROW, DOCS_ROW)), 0.0), axis=0, keepdims=True)
    return down, start_down, finish_down, start_along


def split(value):
    high = value.astype(BF16)
    return high, (value - high.astype(F32)).astype(BF16)


def nt_dot(a, b):
    return lax.dot_general(a, b, (((1,), (1,)), ((), ())), preferred_element_type=F32)


def pool_kernel(
    h_ref, len_ref, partner_ref, w_ref,
    bb_ref, a_ref, ww_ref, loss_ref,
    hv, sb, csend, crecv, rbuf, rs_in, pooled, u, gram, sym,
    load_sem, core_send, core_recv, rs_send, rs_recv, z_send, z_recv, p_send, p_recv, f_send, f_recv,
):
    x = lax.axis_index("dp")
    seq = lax.axis_index("seq")
    chip = lax.div(seq, NCORE)
    core = lax.rem(seq, NCORE)
    z = lax.div(chip, NY)
    y = lax.rem(chip, NY)
    rows = (1 - core, core)

    def device(to_x, to_chip):
        return (to_x, to_chip * NCORE + core)

    def plane_peer(i):
        q = lax.rem(x * NY + y + i, PLANE)
        return device(lax.div(q, NY), z * NY + lax.rem(q, NY))

    other_core = (x, chip * NCORE + 1 - core)

    loads = []
    for o in range(2):
        for q in range(PARTS):
            part = pl.ds(q * (TOK // PARTS), TOK // PARTS)
            copy = pltpu.make_async_copy(
                h_ref.at[rows[o], part], hv.at[o, part], load_sem.at[o * PARTS + q]
            )
            copy.start()
            loads.append(copy)

    barrier = pltpu.get_barrier_semaphore()

    def hello(i, _):
        to = device(x, lax.rem(chip + i, CHIPS))
        pl.semaphore_signal(barrier, inc=1, device_id=to, device_id_type=MESH)
        return 0

    def hello_plane(i, _):
        to = device(lax.rem(x + 1 + lax.div(i, NY), NX), z * NY + lax.rem(y + i, NY))
        pl.semaphore_signal(barrier, inc=1, device_id=to, device_id_type=MESH)
        return 0

    lax.fori_loop(1, CHIPS, hello, 0)
    lax.fori_loop(0, (NX - 1) * NY, hello_plane, 0)
    pl.semaphore_signal(barrier, inc=1, device_id=other_core, device_id_type=MESH)

    def squares(o, q):
        def step(n, _):
            at = pl.ds(pl.multiple_of(q * (TOK // PARTS) + n * 32, 32), 32)
            acc = jnp.zeros((32, 128), F32)
            for t in range(D // 128):
                v = hv[o, at, t * 128 : (t + 1) * 128].astype(F32)
                acc = acc + v * v
            total = jnp.sum(acc, axis=1, keepdims=True)
            sb[o, at, :] = jnp.broadcast_to(lax.rsqrt(total * (1.0 / D) + EPS), (32, 128))
            return 0

        lax.fori_loop(0, TOK // PARTS // 32, step, 0)

    along = (seq * TOK + lax.broadcasted_iota(jnp.int32, (DOCS_ROW, TOK), 1)).astype(F32)

    def selector(o):
        _, start_down, finish_down, _ = bounds(len_ref, rows[o])
        inv = sb[o].T[0:DOCS_ROW, :]
        member = (along >= start_down) & (along < finish_down)
        high, low = split(jnp.where(member, inv, 0.0))
        return jnp.concatenate([high, low], axis=0)

    def sums(chosen, o, q):
        both = jnp.dot(
            chosen, hv[o, :, q * (D // PARTS) : (q + 1) * (D // PARTS)], preferred_element_type=F32
        )
        return both[0:DOCS_ROW] + both[DOCS_ROW : 2 * DOCS_ROW]

    per_part = CHIPS // PARTS
    for q in range(PARTS):
        loads[q].wait()
        squares(0, q)
    chosen = selector(0)
    core_copies = []
    for q in range(PARTS):
        part = sums(chosen, 0, q)
        for b in range(per_part):
            csend[q * per_part + b] = part[:, b * LANES : (b + 1) * LANES]
        if q == 0:
            pl.semaphore_wait(barrier, CHIPS - 1 + (NX - 1) * NY + 1)
        at = pl.ds(q * per_part, per_part)
        copy = pltpu.make_async_remote_copy(
            csend.at[at], crecv.at[at], core_send.at[q], core_recv.at[q],
            device_id=other_core, device_id_type=MESH,
        )
        copy.start()
        core_copies.append(copy)
    for q in range(PARTS):
        loads[PARTS + q].wait()
        squares(1, q)
    chosen = selector(1)
    for q in range(PARTS):
        part = sums(chosen, 1, q)
        core_copies[q].wait()
        for b in range(per_part):
            rbuf[q * per_part + b] = part[:, b * LANES : (b + 1) * LANES] + crecv[q * per_part + b]

        def scatter(b, _):
            @pl.when(b != chip)
            def _():
                pltpu.make_async_remote_copy(
                    rbuf.at[b], rs_in.at[chip], rs_send, rs_recv,
                    device_id=device(x, b), device_id_type=MESH,
                ).start()

            return 0

        lax.fori_loop(q * per_part, (q + 1) * per_part, scatter, 0)

    rs_in[pl.ds(chip, 1)] = rbuf[pl.ds(chip, 1)]
    u[...] = jnp.zeros_like(u)
    gram[...] = jnp.zeros_like(gram)
    lengths, _, _, _ = bounds(len_ref, core)
    pltpu.make_async_remote_copy(
        rbuf.at[pl.ds(0, CHIPS - 1)], rs_in.at[pl.ds(0, CHIPS - 1)], rs_send, rs_recv,
        device_id=other_core, device_id_type=MESH,
    ).wait()
    total = jnp.sum(rs_in[...], axis=0)
    gain = w_ref[:, pl.ds(pl.multiple_of(chip * LANES, LANES), LANES)]
    pooled[chip, x, core] = total * gain / lengths

    def to_planes(dz, _):
        tile = pooled.at[chip, x, core]
        pltpu.make_async_remote_copy(
            tile, tile, z_send, z_recv.at[dz],
            device_id=device(x, lax.rem(z + dz, NZ) * NY + y), device_id_type=MESH,
        ).start()
        return 0

    def to_plane(dz):
        tile = pooled.at[lax.rem(z + NZ - dz, NZ) * NY + y, x, core]

        def step(i, _):
            pltpu.make_async_remote_copy(
                tile, tile, p_send, p_recv.at[dz], device_id=plane_peer(i), device_id_type=MESH
            ).start()
            return 0

        lax.fori_loop(1, PLANE, step, 0)

    lax.fori_loop(1, NZ, to_planes, 0)
    to_plane(0)
    for dz in NEAR_FIRST[1:]:
        tile = pooled.at[lax.rem(z + NZ - dz, NZ) * NY + y, x, core]
        pltpu.make_async_remote_copy(
            tile, tile, z_send, z_recv.at[dz], device_id=other_core, device_id_type=MESH
        ).wait_recv()
        to_plane(dz)

    def forward(dz):
        at = pl.ds(lax.rem(z + NZ - dz, NZ) * NY, NY)
        pltpu.make_async_remote_copy(
            rs_in.at[pl.ds(0, PLANE - 1)], rs_in.at[pl.ds(0, PLANE - 1)], p_send, p_recv.at[dz],
            device_id=other_core, device_id_type=MESH,
        ).wait_recv()
        copy = pltpu.make_async_remote_copy(
            pooled.at[at, :, core], pooled.at[at, :, core], f_send.at[dz], f_recv.at[dz],
            device_id=other_core, device_id_type=MESH,
        )
        copy.start()
        return copy

    def products(dz):
        plane = lax.rem(z + NZ - dz, NZ)
        columns = pl.ds(pl.multiple_of(plane * ZCOLS, ZCOLS), ZCOLS)
        value = jnp.concatenate(
            [pooled[plane * NY + i].reshape(NDOC, LANES) for i in range(NY)], axis=1
        )
        high, low = split(value)
        gram[...] += nt_dot(
            jnp.concatenate([high, high, low], axis=1), jnp.concatenate([high, low, high], axis=1)
        )
        high, low = split(value * w_ref[:, columns])
        both = jnp.concatenate([high, low], axis=0)
        ww_ref[:, columns] = both
        for o in range(2):
            u[o] += nt_dot(hv[o, :, columns], both)

    held = None
    for dz in NEAR_FIRST:
        copy = forward(dz)
        if held is not None:
            held[1].wait()
            products(held[0])
        held = (dz, copy)
    held[1].wait()
    products(held[0])

    k = lax.broadcasted_iota(jnp.int32, (NDOC, NDOC), 0)
    l = lax.broadcasted_iota(jnp.int32, (NDOC, NDOC), 1)
    eye = k == l
    table = gram[...]
    only = jnp.where(eye, table, 0.0)
    norm2 = jnp.sum(only, axis=1, keepdims=True) + EPS
    norms = jnp.sqrt(norm2) * jnp.sqrt(jnp.sum(only, axis=0, keepdims=True) + EPS)
    scaled = 1.0 / (norms * SHARPNESS)
    logits = table * scaled
    weights = jnp.where(eye, 0.0, jnp.exp(logits))
    sum_down = jnp.sum(weights, axis=1, keepdims=True)
    sum_along = jnp.sum(weights, axis=0, keepdims=True)
    pair = jnp.where(partner_ref[...] == k, 1.0, 0.0)
    target = jnp.sum(jnp.sum(pair * logits, axis=1, keepdims=True), axis=0, keepdims=True)
    logs = jnp.sum(jnp.log(sum_down), axis=0, keepdims=True)
    loss_ref[...] = (logs - target) * (1.0 / NDOC)
    change = (weights * (1.0 / sum_down + 1.0 / sum_along) - 2.0 * pair) * (1.0 / NDOC)
    own = jnp.sum(change * logits, axis=1, keepdims=True) / norm2
    sym[...] = change * scaled - jnp.where(eye, own, 0.0)

    place = (seq * TOK + lax.broadcasted_iota(jnp.int32, (TOK, 128), 0)).astype(F32)
    for o in range(2):
        lengths, _, _, start_along = bounds(len_ref, rows[o])
        ours = sym[pl.ds(pl.multiple_of((x * NCORE + rows[o]) * DOCS_ROW, DOCS_ROW), DOCS_ROW), :]
        ours = ours * (LOSS_SCALE / lengths)
        ours = jnp.concatenate([ours, ours], axis=1)
        mix = jnp.broadcast_to(ours[0:1], (TOK, 128))
        for d in range(1, DOCS_ROW):
            mix = jnp.where(place >= start_along[:, d : d + 1], ours[d : d + 1], mix)
        inner = jnp.sum(u[o] * mix, axis=1, keepdims=True) * (1.0 / D)
        inv = sb[o]
        a_ref[rows[o]] = inv * inv * inv * inner
        high, low = split(inv * mix)
        bb_ref[rows[o], :, 0:128] = high
        bb_ref[rows[o], :, 128:256] = low

    pltpu.make_async_copy(rs_in.at[pl.ds(0, NZ - 1)], rs_in.at[pl.ds(0, NZ - 1)], z_send).wait()
    for _ in range(NZ):
        pltpu.make_async_copy(
            rs_in.at[pl.ds(0, PLANE - 1)], rs_in.at[pl.ds(0, PLANE - 1)], p_send
        ).wait()


def grad_kernel(h_ref, bb_ref, a_ref, ww_ref, loss_ref, out_ref, loss_out):
    both = ww_ref[...]
    both = jnp.concatenate([both, both], axis=0)
    for r in range(2):
        for q in range(2):
            at = slice(q * 128, (q + 1) * 128)
            first = jnp.dot(bb_ref[r, at], both, preferred_element_type=F32)
            a = a_ref[r, at]
            a = jnp.concatenate([a] * (first.shape[1] // 128), axis=1)
            out_ref[r, at] = (first - h_ref[r, at].astype(F32) * a).astype(BF16)
    loss_out[...] = loss_ref[...]


def shards(hidden, doc_lengths, partner, closing_layer_weight):
    vmem = pl.BlockSpec(memory_space=pltpu.VMEM)
    dma = pltpu.SemaphoreType.DMA
    bb, a, ww, loss = pl.pallas_call(
        pool_kernel,
        out_shape=(
            jax.ShapeDtypeStruct((2, TOK, 256), BF16),
            jax.ShapeDtypeStruct((2, TOK, 128), F32),
            jax.ShapeDtypeStruct((2 * NDOC, D), BF16),
            jax.ShapeDtypeStruct((1, 1), F32),
        ),
        in_specs=[pl.BlockSpec(memory_space=pltpu.HBM), vmem, vmem, vmem],
        out_specs=(vmem, vmem, vmem, vmem),
        scratch_shapes=[
            pltpu.VMEM((2, TOK, D), BF16),
            pltpu.VMEM((2, TOK, 128), F32),
            pltpu.VMEM((CHIPS, DOCS_ROW, LANES), F32),
            pltpu.VMEM((CHIPS, DOCS_ROW, LANES), F32),
            pltpu.VMEM((CHIPS, DOCS_ROW, LANES), F32),
            pltpu.VMEM((CHIPS, DOCS_ROW, LANES), F32),
            pltpu.VMEM((CHIPS, NX, NCORE, DOCS_ROW, LANES), F32),
            pltpu.VMEM((2, TOK, 128), F32),
            pltpu.VMEM((NDOC, NDOC), F32),
            pltpu.VMEM((NDOC, NDOC), F32),
            dma((2 * PARTS,)),
            dma((PARTS,)), dma((PARTS,)),
            dma, dma,
            dma, dma((NZ,)),
            dma, dma((NZ,)),
            dma((NZ,)), dma((NZ,)),
        ],
        compiler_params=pltpu.CompilerParams(
            collective_id=0, has_side_effects=True, vmem_limit_bytes=20 * 1024 * 1024
        ),
        name="pool_and_loss",
    )(hidden, doc_lengths, partner.reshape(1, NDOC), closing_layer_weight.reshape(1, D))
    width = 512
    out, loss = pl.pallas_call(
        grad_kernel,
        grid=(D // width,),
        out_shape=(
            jax.ShapeDtypeStruct((2, TOK, D), BF16),
            jax.ShapeDtypeStruct((1, 1), F32),
        ),
        in_specs=[
            pl.BlockSpec((2, TOK, width), lambda i: (0, 0, i)),
            pl.BlockSpec((2, TOK, 256), lambda i: (0, 0, 0)),
            pl.BlockSpec((2, TOK, 128), lambda i: (0, 0, 0)),
            pl.BlockSpec((2 * NDOC, width), lambda i: (0, i)),
            pl.BlockSpec((1, 1), lambda i: (0, 0)),
        ],
        out_specs=(
            pl.BlockSpec((2, TOK, width), lambda i: (0, 0, i)),
            pl.BlockSpec((1, 1), lambda i: (0, 0)),
        ),
        compiler_params=pltpu.CompilerParams(vmem_limit_bytes=16 * 1024 * 1024),
        name="hidden_gradient",
    )(hidden, bb, a, ww, loss)
    return out, loss.reshape(())


def solution(mesh):
    in_specs = (P("dp", "seq", None), P("dp", None), P(), P())
    out_specs = (P("dp", "seq", None), P())
    return jax.shard_map(shards, mesh=mesh, in_specs=in_specs, out_specs=out_specs, check_vma=False)
```

time: 255 us -> 48 us (0.19)
  waiting for transfers between devices: 203 us -> 0 us
  Pallas kernels: 0 us -> 42.9 us
  other arithmetic: 18.6 us -> 0 us
  matrix products: 16.6 us -> 0 us
  between operations: 15.9 us -> 0.66 us
  local copies, waits for them, and re-layouts: 1.05 us -> 4.23 us
    psum x1 -> x0, waiting for transfers between devices: 179 us -> none  [shards(): summed = lax.psum(partial_sums, 'seq')]
    pallas_call x0 -> x2, Pallas kernels: none -> 42.9 us  [the longest x1 37.2 us: shards(): pl.pallas_call(pool_kernel, out_shape=(jax.ShapeDtypeStruct((2, TOK, 256)...]
    all_gather x1 -> x0, waiting for transfers between devices: 23.5 us -> none  [shards(): mean_pooled = lax.all_gather(own_mean, 'dp', axis=0, tiled=True)]
    dot_general x4 -> x0, matrix products: 16.6 us -> none  [the longest x1 8.23 us: shards(): jnp.einsum('rdt,rdc->rtc', member.astype(jnp.float32), scaled, precision=...]
    convert_element_type x2 -> x0, other arithmetic: 8.1 us -> none  [the longest x1 7.34 us: shards(): (inv_rms * weighted - float_values * inv_rms ** 3 * inner).astype(jnp.bfl...]
    unnamed x4 -> x10, local copies, waits for them, and re-layouts: 0.01 us -> 4.23 us
    reduce_sum x4 -> x0, other arithmetic: 3.93 us -> none  [the longest x1 3.09 us: shards(): jnp.mean(float_values * float_values, axis=-1, keepdims=True) + 1e-06]
    scatter-add x1 -> x0, other arithmetic: 3.81 us -> none  [contrast(): embedding_lengths = jnp.sqrt(jnp.diagonal(cosine_table) + 1e-06)]
  transfers between devices with their start and end apart: 2 -> 0, of which waited for: 2 -> 0; matrix products, arithmetic and copies ran while one was open for 0% -> 0% of each run, Pallas kernels for 0% -> 0%
where the time goes in v1:
time: 48 us; the launch traced here: 47.8 us
  Pallas kernels  42.9 us (89%)
  local copies, waits for them, and re-layouts  4.23 us (9%)
  between operations  0.66 us (1%)
    pallas_call x1, Pallas kernels, shards(): pl.pallas_call(pool_kernel, out_shape=(jax.ShapeDtypeStruct((2, TOK, 256)...  37.2 us
    pallas_call x1, Pallas kernels, shards(): pl.pallas_call(grad_kernel, grid=(D // width,), out_shape=(jax.ShapeDtype...  5.7 us
    unnamed x10, local copies, waits for them, and re-layouts  4.23 us

profile of v1, /device:TPU:1, one launch (start us, length us, event | category | flops | bytes accessed | tf_op | source)
XLA Modules:
  0.0 47.8 jit_solution(16660851199442012292)
XLA Ops:
  0.6 0.0 copy-start
  0.6 2.2 %copy-done = bf16[2,256,4096]{2,1,0:T(8,128)(2,1)S(1)} copy-done((bf16[2,256,4096]{2,1,0:T(8,128)(2,1)S(1)}, bf16[2,256,4096]{2,1,0:T(8,128)(2,1)}, u32[]{:S(2)}) %copy-start) | copy-done | bytes 4194328
  2.8 0.0 copy-start.2
  2.8 0.7 %copy-done.2 = f32[4096]{0:T(1024)S(1)} copy-done((f32[4096]{0:T(1024)S(1)}, f32[4096]{0:T(1024)}, u32[]{:S(2)}) %copy-start.2) | copy-done | bytes 16408
  3.5 0.0 copy-start.3
  3.5 0.7 %copy-done.3 = s32[2,8]{1,0:T(2,128)S(1)} copy-done((s32[2,8]{1,0:T(2,128)S(1)}, s32[2,8]{1,0:T(2,128)}, u32[]{:S(2)}) %copy-start.3) | copy-done | bytes 88
  4.2 0.0 copy-start.4
  4.2 0.7 %copy-done.4 = s32[64]{0:T(128)S(1)} copy-done((s32[64]{0:T(128)S(1)}, s32[64]{0:T(128)}, u32[]{:S(2)}) %copy-start.4) | copy-done | bytes 280
  4.9 0.0 copy-start.1
  4.9 37.2 %pool_and_loss.1 = (bf16[2,256,256]{2,1,0:T(8,128)(2,1)S(1)}, f32[2,256,128]{2,1,0:T(8,128)S(1)}, bf16[128,4096]{1,0:T(8,128)(2,1)S(1)}, f32[1,1]{1,0:T(1,128)}) custom-call(bf16[2,256,4096]{2,1,0:T(8,128)(2,1)S(1)} %copy-done, s32[2,8]{1,0:T(2,128)S(1)} %copy-done.3, s32[1,64]{1,0:T(1,128)S(1)} %bitcast.4, f32[1,4096]{1,0:T(1,128)S(1)} %bitcast.3), custom_call_target="tpu_custom_call" | custom-call | tf_op jit(solution)/shard_map/pool_and_loss/pallas_call | solution.py:305
  42.1 0.0 copy-done.1
  42.1 5.7 %hidden_gradient.1 = (bf16[2,256,4096]{2,1,0:T(8,128)(2,1)}, f32[1,1]{1,0:T(1,128)}) custom-call(bf16[2,256,4096]{2,1,0:T(8,128)(2,1)S(1)} %copy-done.1, bf16[2,256,256]{2,1,0:T(8,128)(2,1)S(1)} %get-tuple-element.8.bb_ref, f32[2,256,128]{2,1,0:T(8,128)S(1)} %get-tuple-element.9.a_ref, bf16[128,4096]{1,0:T(8,128)(2,1)S(1)} %get-tuple-element.10.ww_ref, ...), custom_call_target="tpu_custom_call" | custom-call | tf_op jit(solution)/shard_map/hidden_gradient/pallas_call | solution.py:339
Async XLA Ops:
  0.6 2.2 %copy-start = (bf16[2,256,4096]{2,1,0:T(8,128)(2,1)S(1)}, bf16[2,256,4096]{2,1,0:T(8,128)(2,1)}, u32[]{:S(2)}) copy-start(bf16[2,256,4096]{2,1,0:T(8,128)(2,1)} %h_ref.3) | copy-start | bytes 12582916
  2.8 0.7 %copy-start.2 = (f32[4096]{0:T(1024)S(1)}, f32[4096]{0:T(1024)}, u32[]{:S(2)}) copy-start(f32[4096]{0:T(1024)} %param.7) | copy-start | bytes 49156
  3.5 0.7 %copy-start.3 = (s32[2,8]{1,0:T(2,128)S(1)}, s32[2,8]{1,0:T(2,128)}, u32[]{:S(2)}) copy-start(s32[2,8]{1,0:T(2,128)} %len_ref.1) | copy-start | bytes 196
  4.2 0.7 %copy-start.4 = (s32[64]{0:T(128)S(1)}, s32[64]{0:T(128)}, u32[]{:S(2)}) copy-start(s32[64]{0:T(128)} %param.6) | copy-start | bytes 772
  4.9 37.2 %copy-start.1 = (bf16[2,256,4096]{2,1,0:T(8,128)(2,1)S(1)}, bf16[2,256,4096]{2,1,0:T(8,128)(2,1)}, u32[]{:S(2)}) copy-start(bf16[2,256,4096]{2,1,0:T(8,128)(2,1)} %h_ref.3) | copy-start | bytes 12582916

commit v2 on v1

--- a/solution.py
+++ b/solution.py
@@ -22,6 +22,7 @@
 LANES = D // CHIPS
 ZCOLS = LANES * NY
 PARTS = 4
+WIDTH = 512
 NEAR_FIRST = (0, 1, 7, 2, 6, 3, 5, 4)
 
 
@@ -47,10 +48,10 @@
 
 
 def pool_kernel(
-    h_ref, len_ref, partner_ref, w_ref,
-    bb_ref, a_ref, ww_ref, loss_ref,
-    hv, sb, csend, crecv, rbuf, rs_in, pooled, u, gram, sym,
-    load_sem, core_send, core_recv, rs_send, rs_recv, z_send, z_recv, p_send, p_recv, f_send, f_recv,
+    h_hbm, len_hbm, partner_hbm, w_hbm,
+    hv, bb_ref, a_ref, ww_ref, loss_ref,
+    len_ref, partner_ref, w_ref, sb, csend, crecv, rbuf, rs_in, pooled, u, gram, sym,
+    load_sem, small_sem, core_send, core_recv, rs_send, rs_recv, z_send, z_recv, p_send, p_recv, f_send, f_recv,
 ):
     x = lax.axis_index("dp")
     seq = lax.axis_index("seq")
@@ -74,10 +75,17 @@
         for q in range(PARTS):
             part = pl.ds(q * (TOK // PARTS), TOK // PARTS)
             copy = pltpu.make_async_copy(
-                h_ref.at[rows[o], part], hv.at[o, part], load_sem.at[o * PARTS + q]
+                h_hbm.at[rows[o], part], hv.at[rows[o], part], load_sem.at[o * PARTS + q]
             )
             copy.start()
             loads.append(copy)
+    small = []
+    for n, (here, there) in enumerate(
+        ((len_hbm, len_ref), (w_hbm, w_ref), (partner_hbm, partner_ref))
+    ):
+        copy = pltpu.make_async_copy(here, there, small_sem.at[n])
+        copy.start()
+        small.append(copy)
 
     barrier = pltpu.get_barrier_semaphore()
 
@@ -100,7 +108,7 @@
             at = pl.ds(pl.multiple_of(q * (TOK // PARTS) + n * 32, 32), 32)
             acc = jnp.zeros((32, 128), F32)
             for t in range(D // 128):
-                v = hv[o, at, t * 128 : (t + 1) * 128].astype(F32)
+                v = hv[rows[o], at, t * 128 : (t + 1) * 128].astype(F32)
                 acc = acc + v * v
             total = jnp.sum(acc, axis=1, keepdims=True)
             sb[o, at, :] = jnp.broadcast_to(lax.rsqrt(total * (1.0 / D) + EPS), (32, 128))
@@ -119,7 +127,7 @@
 
     def sums(chosen, o, q):
         both = jnp.dot(
-            chosen, hv[o, :, q * (D // PARTS) : (q + 1) * (D // PARTS)], preferred_element_type=F32
+            chosen, hv[rows[o], :, q * (D // PARTS) : (q + 1) * (D // PARTS)], preferred_element_type=F32
         )
         return both[0:DOCS_ROW] + both[DOCS_ROW : 2 * DOCS_ROW]
 
@@ -127,6 +135,8 @@
     for q in range(PARTS):
         loads[q].wait()
         squares(0, q)
+    for copy in small:
+        copy.wait()
     chosen = selector(0)
     core_copies = []
     for q in range(PARTS):
@@ -231,7 +241,7 @@
         both = jnp.concatenate([high, low], axis=0)
         ww_ref[:, columns] = both
         for o in range(2):
-            u[o] += nt_dot(hv[o, :, columns], both)
+            u[o] += nt_dot(hv[rows[o], :, columns], both)
 
     held = None
     for dz in NEAR_FIRST:
@@ -286,34 +296,44 @@
         ).wait()
 
 
-def grad_kernel(h_ref, bb_ref, a_ref, ww_ref, loss_ref, out_ref, loss_out):
-    both = ww_ref[...]
-    both = jnp.concatenate([both, both], axis=0)
-    for r in range(2):
-        for q in range(2):
-            at = slice(q * 128, (q + 1) * 128)
-            first = jnp.dot(bb_ref[r, at], both, preferred_element_type=F32)
-            a = a_ref[r, at]
-            a = jnp.concatenate([a] * (first.shape[1] // 128), axis=1)
-            out_ref[r, at] = (first - h_ref[r, at].astype(F32) * a).astype(BF16)
+def grad_kernel(h_ref, bb_ref, a_ref, ww_ref, loss_ref, out_hbm, loss_out, out, sem):
+    copies = []
+    for n in range(D // WIDTH):
+        columns = slice(n * WIDTH, (n + 1) * WIDTH)
+        both = ww_ref[:, columns]
+        both = jnp.concatenate([both, both], axis=0)
+        for r in range(2):
+            first = jnp.dot(bb_ref[r], both, preferred_element_type=F32)
+            a = jnp.concatenate([a_ref[r]] * (WIDTH // 128), axis=1)
+            out[r, :, columns] = (first - h_ref[r, :, columns].astype(F32) * a).astype(BF16)
+        copy = pltpu.make_async_copy(out.at[:, :, columns], out_hbm.at[:, :, columns], sem.at[n])
+        copy.start()
+        copies.append(copy)
     loss_out[...] = loss_ref[...]
+    for copy in copies:
+        copy.wait()
 
 
 def shards(hidden, doc_lengths, partner, closing_layer_weight):
     vmem = pl.BlockSpec(memory_space=pltpu.VMEM)
+    hbm = pl.BlockSpec(memory_space=pltpu.HBM)
     dma = pltpu.SemaphoreType.DMA
-    bb, a, ww, loss = pl.pallas_call(
+    arguments = (hidden, doc_lengths, partner.reshape(1, NDOC), closing_layer_weight.reshape(1, D))
+    h, bb, a, ww, loss = pl.pallas_call(
         pool_kernel,
         out_shape=(
-            jax.ShapeDtypeStruct((2, TOK, 256), BF16),
-            jax.ShapeDtypeStruct((2, TOK, 128), F32),
-            jax.ShapeDtypeStruct((2 * NDOC, D), BF16),
+            pltpu.VMEM((2, TOK, D), BF16),
+            pltpu.VMEM((2, TOK, 256), BF16),
+            pltpu.VMEM((2, TOK, 128), F32),
+            pltpu.VMEM((2 * NDOC, D), BF16),
             jax.ShapeDtypeStruct((1, 1), F32),
         ),
-        in_specs=[pl.BlockSpec(memory_space=pltpu.HBM), vmem, vmem, vmem],
-        out_specs=(vmem, vmem, vmem, vmem),
+        in_specs=[hbm] * 4,
+        out_specs=(vmem,) * 5,
         scratch_shapes=[
-            pltpu.VMEM((2, TOK, D), BF16),
+            pltpu.VMEM((2, DOCS_ROW), jnp.int32),
+            pltpu.VMEM((1, NDOC), jnp.int32),
+            pltpu.VMEM((1, D), F32),
             pltpu.VMEM((2, TOK, 128), F32),
             pltpu.VMEM((CHIPS, DOCS_ROW, LANES), F32),
             pltpu.VMEM((CHIPS, DOCS_ROW, LANES), F32),
@@ -323,7 +343,7 @@
             pltpu.VMEM((2, TOK, 128), F32),
             pltpu.VMEM((NDOC, NDOC), F32),
             pltpu.VMEM((NDOC, NDOC), F32),
-            dma((2 * PARTS,)),
+            dma((2 * PARTS,)), dma((3,)),
             dma((PARTS,)), dma((PARTS,)),
             dma, dma,
             dma, dma((NZ,)),
@@ -331,32 +351,22 @@
             dma((NZ,)), dma((NZ,)),
         ],
         compiler_params=pltpu.CompilerParams(
-            collective_id=0, has_side_effects=True, vmem_limit_bytes=20 * 1024 * 1024
+            collective_id=0, has_side_effects=True, vmem_limit_bytes=16 * 1024 * 1024
         ),
         name="pool_and_loss",
-    )(hidden, doc_lengths, partner.reshape(1, NDOC), closing_layer_weight.reshape(1, D))
-    width = 512
+    )(*(pltpu.with_memory_space_constraint(v, pltpu.HBM) for v in arguments))
     out, loss = pl.pallas_call(
         grad_kernel,
-        grid=(D // width,),
         out_shape=(
             jax.ShapeDtypeStruct((2, TOK, D), BF16),
             jax.ShapeDtypeStruct((1, 1), F32),
         ),
-        in_specs=[
-            pl.BlockSpec((2, TOK, width), lambda i: (0, 0, i)),
-            pl.BlockSpec((2, TOK, 256), lambda i: (0, 0, 0)),
-            pl.BlockSpec((2, TOK, 128), lambda i: (0, 0, 0)),
-            pl.BlockSpec((2 * NDOC, width), lambda i: (0, i)),
-            pl.BlockSpec((1, 1), lambda i: (0, 0)),
-        ],
-        out_specs=(
-            pl.BlockSpec((2, TOK, width), lambda i: (0, 0, i)),
-            pl.BlockSpec((1, 1), lambda i: (0, 0)),
-        ),
+        in_specs=[vmem] * 5,
+        out_specs=(pl.BlockSpec(memory_space=pl.ANY), vmem),
+        scratch_shapes=[pltpu.VMEM((2, TOK, D), BF16), dma((D // WIDTH,))],
         compiler_params=pltpu.CompilerParams(vmem_limit_bytes=16 * 1024 * 1024),
         name="hidden_gradient",
-    )(hidden, bb, a, ww, loss)
+    )(h, bb, a, ww, loss)
     return out, loss.reshape(())
 
 

time: 48 us -> 41.3 us (0.86)
  local copies, waits for them, and re-layouts: 4.23 us -> 0 us
  Pallas kernels: 42.9 us -> 40.6 us
    unnamed x10 -> x0, local copies, waits for them, and re-layouts: 4.23 us -> none
    pallas_call x2, Pallas kernels: 42.9 us -> 40.6 us  [the longest x1 37.1 us: shards(): pl.pallas_call(pool_kernel, out_shape=(pltpu.VMEM((2, TOK, D), BF16), plt...]
where the time goes in v2:
time: 41.3 us; the launch traced here: 41.2 us
  Pallas kernels  40.6 us (98%)
  between operations  0.64 us (2%)
    pallas_call x1, Pallas kernels, shards(): pl.pallas_call(pool_kernel, out_shape=(pltpu.VMEM((2, TOK, D), BF16), plt...  37.1 us
    pallas_call x1, Pallas kernels, shards(): pl.pallas_call(grad_kernel, out_shape=(jax.ShapeDtypeStruct((2, TOK, D),...  3.52 us

profile of v2, /device:TPU:1, one launch (start us, length us, event | category | flops | bytes accessed | tf_op | source)
XLA Modules:
  0.0 41.2 jit_solution(16810687480219059523)
XLA Ops:
  0.6 37.1 %pool_and_loss.1 = (bf16[2,256,4096]{2,1,0:T(8,128)(2,1)S(1)}, bf16[2,256,256]{2,1,0:T(8,128)(2,1)S(1)}, f32[2,256,128]{2,1,0:T(8,128)S(1)}, bf16[128,4096]{1,0:T(8,128)(2,1)S(1)}, f32[1,1]{1,0:T(1,128)}) custom-call(bf16[2,256,4096]{2,1,0:T(8,128)(2,1)} %h_hbm.1, s32[2,8]{1,0:T(2,128)} %len_hbm.1, s32[1,64]{1,0:T(1,128)} %bitcast.4, f32[1,4096]{1,0:T(1,128)} %bitcast.3), custom_call_target="tpu_custom_call" | custom-call | tf_op jit(solution)/shard_map/pool_and_loss/pallas_call | solution.py:322
  37.7 3.5 %hidden_gradient.1 = (bf16[2,256,4096]{2,1,0:T(8,128)(2,1)}, f32[1,1]{1,0:T(1,128)}) custom-call(bf16[2,256,4096]{2,1,0:T(8,128)(2,1)S(1)} %get-tuple-element.9.h_ref, bf16[2,256,256]{2,1,0:T(8,128)(2,1)S(1)} %get-tuple-element.10.bb_ref, f32[2,256,128]{2,1,0:T(8,128)S(1)} %get-tuple-element.11.a_ref, bf16[128,4096]{1,0:T(8,128)(2,1)S(1)} %get-tuple-element.12.ww_ref, ...), custom_call_target="tpu_custom_call" | custom-call | tf_op jit(solution)/shard_map/hidden_gradient/pallas_call | solution.py:358

commit v3 on v2

--- a/solution.py
+++ b/solution.py
@@ -24,6 +24,17 @@
 PARTS = 4
 WIDTH = 512
 NEAR_FIRST = (0, 1, 7, 2, 6, 3, 5, 4)
+BOTH = (3, 5, 4)
+IN_FLIGHT = 8
+
+
+def offsets(dz):
+    found = []
+    for i in range(1, PLANE * NCORE):
+        dx, dy, dc = i // (NY * NCORE), i // NCORE % NY, i % NCORE
+        if dz in BOTH or dc == 0:
+            found.append((dx, dy, dc))
+    return sorted(found, key=lambda t: -min(t[0], NX - t[0]) - min(t[1], NY - t[1]))
 
 
 def bounds(len_ref, row):
@@ -61,12 +72,18 @@
     y = lax.rem(chip, NY)
     rows = (1 - core, core)
 
-    def device(to_x, to_chip):
-        return (to_x, to_chip * NCORE + core)
-
-    def plane_peer(i):
-        q = lax.rem(x * NY + y + i, PLANE)
-        return device(lax.div(q, NY), z * NY + lax.rem(q, NY))
+    def device(to_x, to_chip, to_core=core):
+        return (to_x, to_chip * NCORE + to_core)
+
+    def offset(dx, dz, dy, dc=None):
+        return device(
+            lax.rem(x + dx, NX),
+            lax.rem(z + dz, NZ) * NY + lax.rem(y + dy, NY),
+            lax.rem(core + dc, NCORE) if dc is not None else core,
+        )
+
+    def in_plane(i):
+        return offset(lax.div(i, NY * NCORE), 0, lax.rem(lax.div(i, NCORE), NY), lax.rem(i, NCORE))
 
     other_core = (x, chip * NCORE + 1 - core)
 
@@ -77,8 +94,9 @@
             copy = pltpu.make_async_copy(
                 h_hbm.at[rows[o], part], hv.at[rows[o], part], load_sem.at[o * PARTS + q]
             )
-            copy.start()
             loads.append(copy)
+    for copy in loads[:IN_FLIGHT]:
+        copy.start()
     small = []
     for n, (here, there) in enumerate(
         ((len_hbm, len_ref), (w_hbm, w_ref), (partner_hbm, partner_ref))
@@ -89,63 +107,61 @@
 
     barrier = pltpu.get_barrier_semaphore()
 
-    def hello(i, _):
-        to = device(x, lax.rem(chip + i, CHIPS))
+    def greet(to):
         pl.semaphore_signal(barrier, inc=1, device_id=to, device_id_type=MESH)
+
+    def hello_plane(i, _):
+        greet(in_plane(i))
         return 0
 
-    def hello_plane(i, _):
-        to = device(lax.rem(x + 1 + lax.div(i, NY), NX), z * NY + lax.rem(y + i, NY))
-        pl.semaphore_signal(barrier, inc=1, device_id=to, device_id_type=MESH)
+    def hello_column(i, _):
+        greet(offset(0, lax.div(i, NY), lax.rem(i, NY)))
         return 0
 
-    lax.fori_loop(1, CHIPS, hello, 0)
-    lax.fori_loop(0, (NX - 1) * NY, hello_plane, 0)
-    pl.semaphore_signal(barrier, inc=1, device_id=other_core, device_id_type=MESH)
+    lax.fori_loop(NY, CHIPS, hello_column, 0)
+    lax.fori_loop(1, PLANE * NCORE, hello_plane, 0)
 
     def squares(o, q):
-        def step(n, _):
-            at = pl.ds(pl.multiple_of(q * (TOK // PARTS) + n * 32, 32), 32)
-            acc = jnp.zeros((32, 128), F32)
-            for t in range(D // 128):
-                v = hv[rows[o], at, t * 128 : (t + 1) * 128].astype(F32)
-                acc = acc + v * v
-            total = jnp.sum(acc, axis=1, keepdims=True)
-            sb[o, at, :] = jnp.broadcast_to(lax.rsqrt(total * (1.0 / D) + EPS), (32, 128))
-            return 0
-
-        lax.fori_loop(0, TOK // PARTS // 32, step, 0)
+        n = o * PARTS + q
+        loads[n].wait()
+        if n + IN_FLIGHT < len(loads):
+            loads[n + IN_FLIGHT].start()
+        at = pl.ds(q * (TOK // PARTS), TOK // PARTS)
+        acc = jnp.zeros((TOK // PARTS, 128), F32)
+        for t in range(D // 128):
+            v = hv[rows[o], at, t * 128 : (t + 1) * 128].astype(F32)
+            acc = acc + v * v
+        sb[o, at, :] = acc
 
     along = (seq * TOK + lax.broadcasted_iota(jnp.int32, (DOCS_ROW, TOK), 1)).astype(F32)
 
     def selector(o):
         _, start_down, finish_down, _ = bounds(len_ref, rows[o])
-        inv = sb[o].T[0:DOCS_ROW, :]
+        inv = lax.rsqrt(jnp.sum(sb[o].T, axis=0, keepdims=True) * (1.0 / D) + EPS)
         member = (along >= start_down) & (along < finish_down)
         high, low = split(jnp.where(member, inv, 0.0))
         return jnp.concatenate([high, low], axis=0)
 
-    def sums(chosen, o, q):
-        both = jnp.dot(
-            chosen, hv[rows[o], :, q * (D // PARTS) : (q + 1) * (D // PARTS)], preferred_element_type=F32
-        )
+    def sums(chosen, o, part):
+        columns = pl.ds(pl.multiple_of(part * (D // PARTS), D // PARTS), D // PARTS)
+        both = jnp.dot(chosen, hv[rows[o], :, columns], preferred_element_type=F32)
         return both[0:DOCS_ROW] + both[DOCS_ROW : 2 * DOCS_ROW]
 
     per_part = CHIPS // PARTS
+    order = [lax.rem(lax.div(z * PARTS, NZ) + n, PARTS) for n in (2, 1, 3, 0)]
     for q in range(PARTS):
-        loads[q].wait()
         squares(0, q)
     for copy in small:
         copy.wait()
     chosen = selector(0)
     core_copies = []
-    for q in range(PARTS):
-        part = sums(chosen, 0, q)
+    for q, part in enumerate(order):
+        value = sums(chosen, 0, part)
         for b in range(per_part):
-            csend[q * per_part + b] = part[:, b * LANES : (b + 1) * LANES]
+            csend[part * per_part + b] = value[:, b * LANES : (b + 1) * LANES]
         if q == 0:
-            pl.semaphore_wait(barrier, CHIPS - 1 + (NX - 1) * NY + 1)
-        at = pl.ds(q * per_part, per_part)
+            pl.semaphore_wait(barrier, CHIPS - NY + PLANE * NCORE - 1)
+        at = pl.ds(part * per_part, per_part)
         copy = pltpu.make_async_remote_copy(
             csend.at[at], crecv.at[at], core_send.at[q], core_recv.at[q],
             device_id=other_core, device_id_type=MESH,
@@ -153,28 +169,30 @@
         copy.start()
         core_copies.append(copy)
     for q in range(PARTS):
-        loads[PARTS + q].wait()
         squares(1, q)
     chosen = selector(1)
-    for q in range(PARTS):
-        part = sums(chosen, 1, q)
+    for q, part in enumerate(order):
+        value = sums(chosen, 1, part)
         core_copies[q].wait()
         for b in range(per_part):
-            rbuf[q * per_part + b] = part[:, b * LANES : (b + 1) * LANES] + crecv[q * per_part + b]
-
-        def scatter(b, _):
-            @pl.when(b != chip)
-            def _():
+            to = part * per_part + b
+            rbuf[to] = value[:, b * LANES : (b + 1) * LANES] + crecv[to]
+
+            def scatter(to=to):
                 pltpu.make_async_remote_copy(
-                    rbuf.at[b], rs_in.at[chip], rs_send, rs_recv,
-                    device_id=device(x, b), device_id_type=MESH,
+                    rbuf.at[to], rs_in.at[chip], rs_send, rs_recv,
+                    device_id=device(x, to), device_id_type=MESH,
                 ).start()
 
-            return 0
-
-        lax.fori_loop(q * per_part, (q + 1) * per_part, scatter, 0)
+            if q + 1 < PARTS:
+                scatter()
+            else:
+                pl.when(to != chip)(scatter)
 
     rs_in[pl.ds(chip, 1)] = rbuf[pl.ds(chip, 1)]
+    for o in range(2):
+        square = jnp.sum(sb[o], axis=1, keepdims=True) * (1.0 / D)
+        sb[o] = jnp.broadcast_to(lax.rsqrt(square + EPS), (TOK, 128))
     u[...] = jnp.zeros_like(u)
     gram[...] = jnp.zeros_like(gram)
     lengths, _, _, _ = bounds(len_ref, core)
@@ -186,40 +204,42 @@
     gain = w_ref[:, pl.ds(pl.multiple_of(chip * LANES, LANES), LANES)]
     pooled[chip, x, core] = total * gain / lengths
 
-    def to_planes(dz, _):
-        tile = pooled.at[chip, x, core]
+    mine = pooled.at[chip, x, core]
+
+    def passed(dz):
+        return pooled.at[lax.rem(z + NZ - dz, NZ) * NY + y, x, core]
+
+    def send(tile, dz, to):
         pltpu.make_async_remote_copy(
-            tile, tile, z_send, z_recv.at[dz],
-            device_id=device(x, lax.rem(z + dz, NZ) * NY + y), device_id_type=MESH,
+            tile, tile, p_send, p_recv.at[dz], device_id=to, device_id_type=MESH
         ).start()
-        return 0
 
     def to_plane(dz):
-        tile = pooled.at[lax.rem(z + NZ - dz, NZ) * NY + y, x, core]
-
-        def step(i, _):
-            pltpu.make_async_remote_copy(
-                tile, tile, p_send, p_recv.at[dz], device_id=plane_peer(i), device_id_type=MESH
-            ).start()
-            return 0
-
-        lax.fori_loop(1, PLANE, step, 0)
-
-    lax.fori_loop(1, NZ, to_planes, 0)
+        tile = passed(dz)
+        for dx, dy, dc in offsets(dz):
+            send(tile, dz, offset(dx, 0, dy, dc))
+
+    for dz in NEAR_FIRST[:0:-1]:
+        pltpu.make_async_remote_copy(
+            mine, mine, z_send, z_recv.at[dz], device_id=offset(0, dz, 0), device_id_type=MESH
+        ).start()
     to_plane(0)
     for dz in NEAR_FIRST[1:]:
-        tile = pooled.at[lax.rem(z + NZ - dz, NZ) * NY + y, x, core]
+        tile = passed(dz)
         pltpu.make_async_remote_copy(
             tile, tile, z_send, z_recv.at[dz], device_id=other_core, device_id_type=MESH
         ).wait_recv()
         to_plane(dz)
 
-    def forward(dz):
-        at = pl.ds(lax.rem(z + NZ - dz, NZ) * NY, NY)
+    def take(dz):
+        got = pl.ds(0, PLANE * NCORE - 1 if dz in BOTH else PLANE - 1)
         pltpu.make_async_remote_copy(
-            rs_in.at[pl.ds(0, PLANE - 1)], rs_in.at[pl.ds(0, PLANE - 1)], p_send, p_recv.at[dz],
+            rs_in.at[got], rs_in.at[got], p_send, p_recv.at[dz],
             device_id=other_core, device_id_type=MESH,
         ).wait_recv()
+        if dz in BOTH:
+            return None
+        at = pl.ds(lax.rem(z + NZ - dz, NZ) * NY, NY)
         copy = pltpu.make_async_remote_copy(
             pooled.at[at, :, core], pooled.at[at, :, core], f_send.at[dz], f_recv.at[dz],
             device_id=other_core, device_id_type=MESH,
@@ -243,15 +263,22 @@
         for o in range(2):
             u[o] += nt_dot(hv[rows[o], :, columns], both)
 
-    held = None
+    held = []
     for dz in NEAR_FIRST:
-        copy = forward(dz)
-        if held is not None:
-            held[1].wait()
-            products(held[0])
-        held = (dz, copy)
-    held[1].wait()
-    products(held[0])
+        copy = take(dz)
+        if copy is not None:
+            held.append((dz, copy))
+            if len(held) < 2:
+                continue
+        while len(held) > (copy is not None):
+            first, given = held.pop(0)
+            given.wait()
+            products(first)
+        if copy is None:
+            products(dz)
+    for first, given in held:
+        given.wait()
+        products(first)
 
     k = lax.broadcasted_iota(jnp.int32, (NDOC, NDOC), 0)
     l = lax.broadcasted_iota(jnp.int32, (NDOC, NDOC), 1)
@@ -290,14 +317,16 @@
         bb_ref[rows[o], :, 128:256] = low
 
     pltpu.make_async_copy(rs_in.at[pl.ds(0, NZ - 1)], rs_in.at[pl.ds(0, NZ - 1)], z_send).wait()
-    for _ in range(NZ):
-        pltpu.make_async_copy(
-            rs_in.at[pl.ds(0, PLANE - 1)], rs_in.at[pl.ds(0, PLANE - 1)], p_send
-        ).wait()
+    left = sum(len(offsets(dz)) for dz in NEAR_FIRST)
+    while left:
+        some = pl.ds(0, min(left, CHIPS))
+        pltpu.make_async_copy(rs_in.at[some], rs_in.at[some], p_send).wait()
+        left -= min(left, CHIPS)
 
 
 def grad_kernel(h_ref, bb_ref, a_ref, ww_ref, loss_ref, out_hbm, loss_out, out, sem):
-    copies = []
+    copies = [pltpu.make_async_copy(loss_ref, loss_out, sem.at[D // WIDTH])]
+    copies[0].start()
     for n in range(D // WIDTH):
         columns = slice(n * WIDTH, (n + 1) * WIDTH)
         both = ww_ref[:, columns]
@@ -309,7 +338,6 @@
         copy = pltpu.make_async_copy(out.at[:, :, columns], out_hbm.at[:, :, columns], sem.at[n])
         copy.start()
         copies.append(copy)
-    loss_out[...] = loss_ref[...]
     for copy in copies:
         copy.wait()
 
@@ -326,7 +354,7 @@
             pltpu.VMEM((2, TOK, 256), BF16),
             pltpu.VMEM((2, TOK, 128), F32),
             pltpu.VMEM((2 * NDOC, D), BF16),
-            jax.ShapeDtypeStruct((1, 1), F32),
+            pltpu.VMEM((1, 1), F32),
         ),
         in_specs=[hbm] * 4,
         out_specs=(vmem,) * 5,
@@ -362,8 +390,8 @@
             jax.ShapeDtypeStruct((1, 1), F32),
         ),
         in_specs=[vmem] * 5,
-        out_specs=(pl.BlockSpec(memory_space=pl.ANY), vmem),
-        scratch_shapes=[pltpu.VMEM((2, TOK, D), BF16), dma((D // WIDTH,))],
+        out_specs=(pl.BlockSpec(memory_space=pl.ANY),) * 2,
+        scratch_shapes=[pltpu.VMEM((2, TOK, D), BF16), dma((D // WIDTH + 1,))],
         compiler_params=pltpu.CompilerParams(vmem_limit_bytes=16 * 1024 * 1024),
         name="hidden_gradient",
     )(h, bb, a, ww, loss)

time: 41.3 us -> 38.4 us (0.930)
  Pallas kernels: 40.6 us -> 37.7 us
    pallas_call x1, Pallas kernels: 37.1 us -> 34.7 us  [shards(): pl.pallas_call(pool_kernel, out_shape=(pltpu.VMEM((2, TOK, D), BF16), plt...]
    pallas_call x1, Pallas kernels: 3.52 us -> 3.02 us  [shards(): pl.pallas_call(grad_kernel, out_shape=(jax.ShapeDtypeStruct((2, TOK, D),...]
where the time goes in v3:
time: 38.4 us; the launch traced here: 38.3 us
  Pallas kernels  37.7 us (98%)
  between operations  0.64 us (2%)
    pallas_call x1, Pallas kernels, shards(): pl.pallas_call(pool_kernel, out_shape=(pltpu.VMEM((2, TOK, D), BF16), plt...  34.7 us
    pallas_call x1, Pallas kernels, shards(): pl.pallas_call(grad_kernel, out_shape=(jax.ShapeDtypeStruct((2, TOK, D),...  3.02 us

profile of v3, /device:TPU:1, one launch (start us, length us, event | category | flops | bytes accessed | tf_op | source)
XLA Modules:
  0.0 38.3 jit_solution(10326525502875156095)
XLA Ops:
  0.6 34.7 %pool_and_loss.1 = (bf16[2,256,4096]{2,1,0:T(8,128)(2,1)S(1)}, bf16[2,256,256]{2,1,0:T(8,128)(2,1)S(1)}, f32[2,256,128]{2,1,0:T(8,128)S(1)}, bf16[128,4096]{1,0:T(8,128)(2,1)S(1)}, f32[1,1]{1,0:T(1,128)}) custom-call(bf16[2,256,4096]{2,1,0:T(8,128)(2,1)} %h_hbm.1, s32[2,8]{1,0:T(2,128)} %len_hbm.1, s32[1,64]{1,0:T(1,128)} %bitcast.4, f32[1,4096]{1,0:T(1,128)} %bitcast.3), custom_call_target="tpu_custom_call" | custom-call | tf_op jit(solution)/shard_map/pool_and_loss/pallas_call | solution.py:350
  35.3 3.0 %hidden_gradient.1 = (bf16[2,256,4096]{2,1,0:T(8,128)(2,1)}, f32[1,1]{1,0:T(1,128)}) custom-call(bf16[2,256,4096]{2,1,0:T(8,128)(2,1)S(1)} %get-tuple-element.9.h_ref, bf16[2,256,256]{2,1,0:T(8,128)(2,1)S(1)} %get-tuple-element.10.bb_ref, f32[2,256,128]{2,1,0:T(8,128)S(1)} %get-tuple-element.11.a_ref, bf16[128,4096]{1,0:T(8,128)(2,1)S(1)} %get-tuple-element.12.ww_ref, ...), custom_call_target="tpu_custom_call" | custom-call | tf_op jit(solution)/shard_map/hidden_gradient/pallas_call | solution.py:386

commit v4 on v3

--- a/solution.py
+++ b/solution.py
@@ -23,8 +23,10 @@
 ZCOLS = LANES * NY
 PARTS = 4
 WIDTH = 512
-NEAR_FIRST = (0, 1, 7, 2, 6, 3, 5, 4)
-BOTH = (3, 5, 4)
+BOTH = (4, 3)
+WHOLE = (1, 7)
+RELAYED = (2, 6, 3, 5, 4)
+TAKEN = (0, 2, 6, 1, 7, 3, 5, 4)
 IN_FLIGHT = 8
 
 
@@ -35,6 +37,20 @@
         if dz in BOTH or dc == 0:
             found.append((dx, dy, dc))
     return sorted(found, key=lambda t: -min(t[0], NX - t[0]) - min(t[1], NY - t[1]))
+
+
+def peers():
+    found = [(dz, 0, dy, 0) for dz in range(1, NZ) for dy in range(NY)]
+    found += [(0, *at) for at in offsets(BOTH[0])] + [(dz, 0, 0, 1) for dz in WHOLE]
+
+    def hops(t):
+        return min(t[0], NZ - t[0]) + min(t[1], NX - t[1]) + min(t[2], NY - t[2])
+
+    return sorted(found, key=lambda t: -hops(t))
+
+
+PEERS = peers()
+NEXT = 16
 
 
 def bounds(len_ref, row):
@@ -62,7 +78,7 @@
     h_hbm, len_hbm, partner_hbm, w_hbm,
     hv, bb_ref, a_ref, ww_ref, loss_ref,
     len_ref, partner_ref, w_ref, sb, csend, crecv, rbuf, rs_in, pooled, u, gram, sym,
-    load_sem, small_sem, core_send, core_recv, rs_send, rs_recv, z_send, z_recv, p_send, p_recv, f_send, f_recv,
+    load_sem, small_sem, core_send, core_recv, rs_send, rs_recv, z_send, z_recv, p_send, p_recv, f_send, f_recv, n_send,
 ):
     x = lax.axis_index("dp")
     seq = lax.axis_index("seq")
@@ -82,11 +98,23 @@
             lax.rem(core + dc, NCORE) if dc is not None else core,
         )
 
-    def in_plane(i):
-        return offset(lax.div(i, NY * NCORE), 0, lax.rem(lax.div(i, NCORE), NY), lax.rem(i, NCORE))
-
     other_core = (x, chip * NCORE + 1 - core)
 
+    barrier = pltpu.get_barrier_semaphore()
+
+    def greet(to):
+        pl.semaphore_signal(barrier, inc=1, device_id=to, device_id_type=MESH)
+
+    for dz, dx, dy, dc in PEERS[:NEXT]:
+        greet(offset(dx, dz, dy, dc))
+
+    small = []
+    for n, (here, there) in enumerate(
+        ((len_hbm, len_ref), (w_hbm, w_ref), (partner_hbm, partner_ref))
+    ):
+        copy = pltpu.make_async_copy(here, there, small_sem.at[n])
+        copy.start()
+        small.append(copy)
     loads = []
     for o in range(2):
         for q in range(PARTS):
@@ -97,29 +125,9 @@
             loads.append(copy)
     for copy in loads[:IN_FLIGHT]:
         copy.start()
-    small = []
-    for n, (here, there) in enumerate(
-        ((len_hbm, len_ref), (w_hbm, w_ref), (partner_hbm, partner_ref))
-    ):
-        copy = pltpu.make_async_copy(here, there, small_sem.at[n])
-        copy.start()
-        small.append(copy)
-
-    barrier = pltpu.get_barrier_semaphore()
-
-    def greet(to):
-        pl.semaphore_signal(barrier, inc=1, device_id=to, device_id_type=MESH)
-
-    def hello_plane(i, _):
-        greet(in_plane(i))
-        return 0
-
-    def hello_column(i, _):
-        greet(offset(0, lax.div(i, NY), lax.rem(i, NY)))
-        return 0
-
-    lax.fori_loop(NY, CHIPS, hello_column, 0)
-    lax.fori_loop(1, PLANE * NCORE, hello_plane, 0)
+
+    for dz, dx, dy, dc in PEERS[NEXT:]:
+        greet(offset(dx, dz, dy, dc))
 
     def squares(o, q):
         n = o * PARTS + q
@@ -154,13 +162,20 @@
     for copy in small:
         copy.wait()
     chosen = selector(0)
-    core_copies = []
-    for q, part in enumerate(order):
+    for part in order:
         value = sums(chosen, 0, part)
         for b in range(per_part):
             csend[part * per_part + b] = value[:, b * LANES : (b + 1) * LANES]
-        if q == 0:
-            pl.semaphore_wait(barrier, CHIPS - NY + PLANE * NCORE - 1)
+    for q in range(PARTS):
+        squares(1, q)
+    chosen = selector(1)
+    for part in order:
+        value = sums(chosen, 1, part)
+        for b in range(per_part):
+            rbuf[part * per_part + b] = value[:, b * LANES : (b + 1) * LANES]
+    pl.semaphore_wait(barrier, len(PEERS))
+    core_copies = []
+    for q, part in enumerate(order):
         at = pl.ds(part * per_part, per_part)
         copy = pltpu.make_async_remote_copy(
             csend.at[at], crecv.at[at], core_send.at[q], core_recv.at[q],
@@ -168,15 +183,12 @@
         )
         copy.start()
         core_copies.append(copy)
-    for q in range(PARTS):
-        squares(1, q)
-    chosen = selector(1)
     for q, part in enumerate(order):
-        value = sums(chosen, 1, part)
-        core_copies[q].wait()
+        core_copies[q].wait_recv()
+        at = pl.ds(part * per_part, per_part)
+        rbuf[at] = rbuf[at] + crecv[at]
         for b in range(per_part):
             to = part * per_part + b
-            rbuf[to] = value[:, b * LANES : (b + 1) * LANES] + crecv[to]
 
             def scatter(to=to):
                 pltpu.make_async_remote_copy(
@@ -188,6 +200,8 @@
                 scatter()
             else:
                 pl.when(to != chip)(scatter)
+    for copy in core_copies:
+        copy.wait_send()
 
     rs_in[pl.ds(chip, 1)] = rbuf[pl.ds(chip, 1)]
     for o in range(2):
@@ -219,12 +233,12 @@
         for dx, dy, dc in offsets(dz):
             send(tile, dz, offset(dx, 0, dy, dc))
 
-    for dz in NEAR_FIRST[:0:-1]:
+    for dz in RELAYED[::-1]:
         pltpu.make_async_remote_copy(
             mine, mine, z_send, z_recv.at[dz], device_id=offset(0, dz, 0), device_id_type=MESH
         ).start()
     to_plane(0)
-    for dz in NEAR_FIRST[1:]:
+    for dz in RELAYED:
         tile = passed(dz)
         pltpu.make_async_remote_copy(
             tile, tile, z_send, z_recv.at[dz], device_id=other_core, device_id_type=MESH
@@ -232,12 +246,13 @@
         to_plane(dz)
 
     def take(dz):
-        got = pl.ds(0, PLANE * NCORE - 1 if dz in BOTH else PLANE - 1)
+        parts = PLANE * NCORE if dz in WHOLE else PLANE * NCORE - 1 if dz in BOTH else PLANE - 1
+        got = pl.ds(0, parts)
         pltpu.make_async_remote_copy(
             rs_in.at[got], rs_in.at[got], p_send, p_recv.at[dz],
             device_id=other_core, device_id_type=MESH,
         ).wait_recv()
-        if dz in BOTH:
+        if dz in BOTH or dz in WHOLE:
             return None
         at = pl.ds(lax.rem(z + NZ - dz, NZ) * NY, NY)
         copy = pltpu.make_async_remote_copy(
@@ -245,6 +260,13 @@
             device_id=other_core, device_id_type=MESH,
         )
         copy.start()
+        if dz == 0:
+            for to in WHOLE:
+                for dc in range(NCORE):
+                    pltpu.make_async_remote_copy(
+                        pooled.at[at, :, core], pooled.at[at, :, core], n_send, p_recv.at[to],
+                        device_id=offset(0, to, 0, dc), device_id_type=MESH,
+                    ).start()
         return copy
 
     def products(dz):
@@ -264,7 +286,7 @@
             u[o] += nt_dot(hv[rows[o], :, columns], both)
 
     held = []
-    for dz in NEAR_FIRST:
+    for dz in TAKEN:
         copy = take(dz)
         if copy is not None:
             held.append((dz, copy))
@@ -316,8 +338,12 @@
         bb_ref[rows[o], :, 0:128] = high
         bb_ref[rows[o], :, 128:256] = low
 
-    pltpu.make_async_copy(rs_in.at[pl.ds(0, NZ - 1)], rs_in.at[pl.ds(0, NZ - 1)], z_send).wait()
-    left = sum(len(offsets(dz)) for dz in NEAR_FIRST)
+    some = pl.ds(0, len(RELAYED))
+    pltpu.make_async_copy(rs_in.at[some], rs_in.at[some], z_send).wait()
+    for _ in range(2 * len(WHOLE)):
+        some = pl.ds(0, PLANE)
+        pltpu.make_async_copy(rs_in.at[some], rs_in.at[some], n_send).wait()
+    left = sum(len(offsets(dz)) for dz in (0, *RELAYED))
     while left:
         some = pl.ds(0, min(left, CHIPS))
         pltpu.make_async_copy(rs_in.at[some], rs_in.at[some], p_send).wait()
@@ -377,6 +403,7 @@
             dma, dma((NZ,)),
             dma, dma((NZ,)),
             dma((NZ,)), dma((NZ,)),
+            dma,
         ],
         compiler_params=pltpu.CompilerParams(
             collective_id=0, has_side_effects=True, vmem_limit_bytes=16 * 1024 * 1024

time: 38.4 us -> 37.1 us (0.966)
  Pallas kernels: 37.7 us -> 36.4 us
    pallas_call x1, Pallas kernels: 34.7 us -> 33.4 us  [shards(): pl.pallas_call(pool_kernel, out_shape=(pltpu.VMEM((2, TOK, D), BF16), plt...]
where the time goes in v4:
time: 37.1 us; the launch traced here: 37 us
  Pallas kernels  36.4 us (98%)
  between operations  0.64 us (2%)
    pallas_call x1, Pallas kernels, shards(): pl.pallas_call(pool_kernel, out_shape=(pltpu.VMEM((2, TOK, D), BF16), plt...  33.4 us
    pallas_call x1, Pallas kernels, shards(): pl.pallas_call(grad_kernel, out_shape=(jax.ShapeDtypeStruct((2, TOK, D),...  3.02 us

profile of v4, /device:TPU:1, one launch (start us, length us, event | category | flops | bytes accessed | tf_op | source)
XLA Modules:
  0.0 37.0 jit_solution(1990827247410019846)
XLA Ops:
  0.6 33.4 %pool_and_loss.1 = (bf16[2,256,4096]{2,1,0:T(8,128)(2,1)S(1)}, bf16[2,256,256]{2,1,0:T(8,128)(2,1)S(1)}, f32[2,256,128]{2,1,0:T(8,128)S(1)}, bf16[128,4096]{1,0:T(8,128)(2,1)S(1)}, f32[1,1]{1,0:T(1,128)}) custom-call(bf16[2,256,4096]{2,1,0:T(8,128)(2,1)} %h_hbm.1, s32[2,8]{1,0:T(2,128)} %len_hbm.1, s32[1,64]{1,0:T(1,128)} %bitcast.4, f32[1,4096]{1,0:T(1,128)} %bitcast.3), custom_call_target="tpu_custom_call" | custom-call | tf_op jit(solution)/shard_map/pool_and_loss/pallas_call | solution.py:376
  34.0 3.0 %hidden_gradient.1 = (bf16[2,256,4096]{2,1,0:T(8,128)(2,1)}, f32[1,1]{1,0:T(1,128)}) custom-call(bf16[2,256,4096]{2,1,0:T(8,128)(2,1)S(1)} %get-tuple-element.9.h_ref, bf16[2,256,256]{2,1,0:T(8,128)(2,1)S(1)} %get-tuple-element.10.bb_ref, f32[2,256,128]{2,1,0:T(8,128)S(1)} %get-tuple-element.11.a_ref, bf16[128,4096]{1,0:T(8,128)(2,1)S(1)} %get-tuple-element.12.ww_ref, ...), custom_call_target="tpu_custom_call" | custom-call | tf_op jit(solution)/shard_map/hidden_gradient/pallas_call | solution.py:413

commit v5 on v4

--- a/solution.py
+++ b/solution.py
@@ -22,8 +22,8 @@
 LANES = D // CHIPS
 ZCOLS = LANES * NY
 PARTS = 4
-WIDTH = 512
-BOTH = (4, 3)
+WIDTHS = (256, 256, 512, 512, 512, 512, 512, 512, 256, 256)
+BOTH = (4,)
 WHOLE = (1, 7)
 RELAYED = (2, 6, 3, 5, 4)
 TAKEN = (0, 2, 6, 1, 7, 3, 5, 4)
@@ -269,7 +269,7 @@
                     ).start()
         return copy
 
-    def products(dz):
+    def products(dz, last=False):
         plane = lax.rem(z + NZ - dz, NZ)
         columns = pl.ds(pl.multiple_of(plane * ZCOLS, ZCOLS), ZCOLS)
         value = jnp.concatenate(
@@ -281,9 +281,15 @@
         )
         high, low = split(value * w_ref[:, columns])
         both = jnp.concatenate([high, low], axis=0)
-        ww_ref[:, columns] = both
-        for o in range(2):
-            u[o] += nt_dot(hv[rows[o], :, columns], both)
+
+        def inner():
+            ww_ref[:, columns] = both
+            for o in range(2):
+                u[o] += nt_dot(hv[rows[o], :, columns], both)
+
+        if last:
+            return inner
+        inner()
 
     held = []
     for dz in TAKEN:
@@ -297,10 +303,7 @@
             given.wait()
             products(first)
         if copy is None:
-            products(dz)
-    for first, given in held:
-        given.wait()
-        products(first)
+            rest = products(dz, dz == TAKEN[-1])
 
     k = lax.broadcasted_iota(jnp.int32, (NDOC, NDOC), 0)
     l = lax.broadcasted_iota(jnp.int32, (NDOC, NDOC), 1)
@@ -322,6 +325,8 @@
     own = jnp.sum(change * logits, axis=1, keepdims=True) / norm2
     sym[...] = change * scaled - jnp.where(eye, own, 0.0)
 
+    rest()
+
     place = (seq * TOK + lax.broadcasted_iota(jnp.int32, (TOK, 128), 0)).astype(F32)
     for o in range(2):
         lengths, _, _, start_along = bounds(len_ref, rows[o])
@@ -351,15 +356,15 @@
 
 
 def grad_kernel(h_ref, bb_ref, a_ref, ww_ref, loss_ref, out_hbm, loss_out, out, sem):
-    copies = [pltpu.make_async_copy(loss_ref, loss_out, sem.at[D // WIDTH])]
+    copies = [pltpu.make_async_copy(loss_ref, loss_out, sem.at[len(WIDTHS)])]
     copies[0].start()
-    for n in range(D // WIDTH):
-        columns = slice(n * WIDTH, (n + 1) * WIDTH)
+    for n, width in enumerate(WIDTHS):
+        columns = slice(sum(WIDTHS[:n]), sum(WIDTHS[: n + 1]))
         both = ww_ref[:, columns]
         both = jnp.concatenate([both, both], axis=0)
         for r in range(2):
             first = jnp.dot(bb_ref[r], both, preferred_element_type=F32)
-            a = jnp.concatenate([a_ref[r]] * (WIDTH // 128), axis=1)
+            a = jnp.concatenate([a_ref[r]] * (width // 128), axis=1)
             out[r, :, columns] = (first - h_ref[r, :, columns].astype(F32) * a).astype(BF16)
         copy = pltpu.make_async_copy(out.at[:, :, columns], out_hbm.at[:, :, columns], sem.at[n])
         copy.start()
@@ -418,7 +423,7 @@
         ),
         in_specs=[vmem] * 5,
         out_specs=(pl.BlockSpec(memory_space=pl.ANY),) * 2,
-        scratch_shapes=[pltpu.VMEM((2, TOK, D), BF16), dma((D // WIDTH + 1,))],
+        scratch_shapes=[pltpu.VMEM((2, TOK, D), BF16), dma((len(WIDTHS) + 1,))],
         compiler_params=pltpu.CompilerParams(vmem_limit_bytes=16 * 1024 * 1024),
         name="hidden_gradient",
     )(h, bb, a, ww, loss)

time: 37.1 us -> 36.8 us (level)
  no operation moved by 1% of the time
where the time goes in v5:
time: 36.8 us; the launch traced here: 36.7 us
  Pallas kernels  36.1 us (98%)
  between operations  0.64 us (2%)
    pallas_call x1, Pallas kernels, shards(): pl.pallas_call(pool_kernel, out_shape=(pltpu.VMEM((2, TOK, D), BF16), plt...  33.1 us
    pallas_call x1, Pallas kernels, shards(): pl.pallas_call(grad_kernel, out_shape=(jax.ShapeDtypeStruct((2, TOK, D),...  3 us

profile of v5, /device:TPU:1, one launch (start us, length us, event | category | flops | bytes accessed | tf_op | source)
XLA Modules:
  0.0 36.7 jit_solution(7332662617853316455)
XLA Ops:
  0.6 33.1 %pool_and_loss.1 = (bf16[2,256,4096]{2,1,0:T(8,128)(2,1)S(1)}, bf16[2,256,256]{2,1,0:T(8,128)(2,1)S(1)}, f32[2,256,128]{2,1,0:T(8,128)S(1)}, bf16[128,4096]{1,0:T(8,128)(2,1)S(1)}, f32[1,1]{1,0:T(1,128)}) custom-call(bf16[2,256,4096]{2,1,0:T(8,128)(2,1)} %h_hbm.1, s32[2,8]{1,0:T(2,128)} %len_hbm.1, s32[1,64]{1,0:T(1,128)} %bitcast.4, f32[1,4096]{1,0:T(1,128)} %bitcast.3), custom_call_target="tpu_custom_call" | custom-call | tf_op jit(solution)/shard_map/pool_and_loss/pallas_call | solution.py:381
  33.7 3.0 %hidden_gradient.1 = (bf16[2,256,4096]{2,1,0:T(8,128)(2,1)}, f32[1,1]{1,0:T(1,128)}) custom-call(bf16[2,256,4096]{2,1,0:T(8,128)(2,1)S(1)} %get-tuple-element.9.h_ref, bf16[2,256,256]{2,1,0:T(8,128)(2,1)S(1)} %get-tuple-element.10.bb_ref, f32[2,256,128]{2,1,0:T(8,128)S(1)} %get-tuple-element.11.a_ref, bf16[128,4096]{1,0:T(8,128)(2,1)S(1)} %get-tuple-element.12.ww_ref, ...), custom_call_target="tpu_custom_call" | custom-call | tf_op jit(solution)/shard_map/hidden_gradient/pallas_call | solution.py:418

commit v6 on v5

--- a/solution.py
+++ b/solution.py
@@ -188,7 +188,8 @@
         at = pl.ds(part * per_part, per_part)
         rbuf[at] = rbuf[at] + crecv[at]
         for b in range(per_part):
-            to = part * per_part + b
+            along_y = lax.rem(y + (2, 1, 3, 0)[b // (NZ // PARTS)], NY)
+            to = part * per_part + b % (NZ // PARTS) * NY + along_y
 
             def scatter(to=to):
                 pltpu.make_async_remote_copy(

time: 36.8 us -> 36.5 us (level)
  no operation moved by 1% of the time
where the time goes in v6:
time: 36.5 us; the launch traced here: 36.4 us
  Pallas kernels  35.8 us (98%)
  between operations  0.64 us (2%)
    pallas_call x1, Pallas kernels, shards(): pl.pallas_call(pool_kernel, out_shape=(pltpu.VMEM((2, TOK, D), BF16), plt...  32.8 us
    pallas_call x1, Pallas kernels, shards(): pl.pallas_call(grad_kernel, out_shape=(jax.ShapeDtypeStruct((2, TOK, D),...  3 us

profile of v6, /device:TPU:1, one launch (start us, length us, event | category | flops | bytes accessed | tf_op | source)
XLA Modules:
  0.0 36.4 jit_solution(12884884204476928600)
XLA Ops:
  0.6 32.8 %pool_and_loss.1 = (bf16[2,256,4096]{2,1,0:T(8,128)(2,1)S(1)}, bf16[2,256,256]{2,1,0:T(8,128)(2,1)S(1)}, f32[2,256,128]{2,1,0:T(8,128)S(1)}, bf16[128,4096]{1,0:T(8,128)(2,1)S(1)}, f32[1,1]{1,0:T(1,128)}) custom-call(bf16[2,256,4096]{2,1,0:T(8,128)(2,1)} %h_hbm.1, s32[2,8]{1,0:T(2,128)} %len_hbm.1, s32[1,64]{1,0:T(1,128)} %bitcast.4, f32[1,4096]{1,0:T(1,128)} %bitcast.3), custom_call_target="tpu_custom_call" | custom-call | tf_op jit(solution)/shard_map/pool_and_loss/pallas_call | solution.py:382
  33.4 3.0 %hidden_gradient.1 = (bf16[2,256,4096]{2,1,0:T(8,128)(2,1)}, f32[1,1]{1,0:T(1,128)}) custom-call(bf16[2,256,4096]{2,1,0:T(8,128)(2,1)S(1)} %get-tuple-element.9.h_ref, bf16[2,256,256]{2,1,0:T(8,128)(2,1)S(1)} %get-tuple-element.10.bb_ref, f32[2,256,128]{2,1,0:T(8,128)S(1)} %get-tuple-element.11.a_ref, bf16[128,4096]{1,0:T(8,128)(2,1)S(1)} %get-tuple-element.12.ww_ref, ...), custom_call_target="tpu_custom_call" | custom-call | tf_op jit(solution)/shard_map/hidden_gradient/pallas_call | solution.py:419

commit v7 on v6

--- a/solution.py
+++ b/solution.py
@@ -260,7 +260,6 @@
             pooled.at[at, :, core], pooled.at[at, :, core], f_send.at[dz], f_recv.at[dz],
             device_id=other_core, device_id_type=MESH,
         )
-        copy.start()
         if dz == 0:
             for to in WHOLE:
                 for dc in range(NCORE):
@@ -268,6 +267,7 @@
                         pooled.at[at, :, core], pooled.at[at, :, core], n_send, p_recv.at[to],
                         device_id=offset(0, to, 0, dc), device_id_type=MESH,
                     ).start()
+        copy.start()
         return copy
 
     def products(dz, last=False):

time: 36.5 us -> 36.5 us (level)
  no operation moved by 1% of the time
where the time goes in v7:
time: 36.5 us; the launch traced here: 36.4 us
  Pallas kernels  35.8 us (98%)
  between operations  0.64 us (2%)
    pallas_call x1, Pallas kernels, shards(): pl.pallas_call(pool_kernel, out_shape=(pltpu.VMEM((2, TOK, D), BF16), plt...  32.8 us
    pallas_call x1, Pallas kernels, shards(): pl.pallas_call(grad_kernel, out_shape=(jax.ShapeDtypeStruct((2, TOK, D),...  3 us

profile of v7, /device:TPU:1, one launch (start us, length us, event | category | flops | bytes accessed | tf_op | source)
XLA Modules:
  0.0 36.4 jit_solution(10752517001908521144)
XLA Ops:
  0.6 32.8 %pool_and_loss.1 = (bf16[2,256,4096]{2,1,0:T(8,128)(2,1)S(1)}, bf16[2,256,256]{2,1,0:T(8,128)(2,1)S(1)}, f32[2,256,128]{2,1,0:T(8,128)S(1)}, bf16[128,4096]{1,0:T(8,128)(2,1)S(1)}, f32[1,1]{1,0:T(1,128)}) custom-call(bf16[2,256,4096]{2,1,0:T(8,128)(2,1)} %h_hbm.1, s32[2,8]{1,0:T(2,128)} %len_hbm.1, s32[1,64]{1,0:T(1,128)} %bitcast.4, f32[1,4096]{1,0:T(1,128)} %bitcast.3), custom_call_target="tpu_custom_call" | custom-call | tf_op jit(solution)/shard_map/pool_and_loss/pallas_call | solution.py:382
  33.4 3.0 %hidden_gradient.1 = (bf16[2,256,4096]{2,1,0:T(8,128)(2,1)}, f32[1,1]{1,0:T(1,128)}) custom-call(bf16[2,256,4096]{2,1,0:T(8,128)(2,1)S(1)} %get-tuple-element.9.h_ref, bf16[2,256,256]{2,1,0:T(8,128)(2,1)S(1)} %get-tuple-element.10.bb_ref, f32[2,256,128]{2,1,0:T(8,128)S(1)} %get-tuple-element.11.a_ref, bf16[128,4096]{1,0:T(8,128)(2,1)S(1)} %get-tuple-element.12.ww_ref, ...), custom_call_target="tpu_custom_call" | custom-call | tf_op jit(solution)/shard_map/hidden_gradient/pallas_call | solution.py:419
